TPU v7x, 128 devices: a whole 4x4x4 slice. The times are simulated.
128 devices in a mesh: row: 8 (over z, core), col: 16 (over x, y).
Axes of the slice: x: 4, y: 4, z: 4, core: 2. Of those that a mesh axis runs over, the one named last changes fastest.
Arguments:
- front_panel: float32 [40960, 512], P('row', 'col'), may hold values from -16 to 48, as said below
- front_slab: float32 [40960, 8192], P('row', 'col'), may hold values from -6 to 6
- child_one: bfloat16 [8192, 8192], P('col', 'row'), may hold values from -6 to 6
- child_two: bfloat16 [8192, 8192], P('col', 'row'), may hold values from -6 to 6
- map_one: int32 [32], replicated, may hold values from 0 to 159, as said below
- map_two: int32 [32], replicated, may hold values from 0 to 159, as said below
Outputs:
- factor_panel: float32 [40960, 512], P('row', 'col')
- slab_out: float32 [40960, 8192], P('row', 'col')
Inputs may be any that keep to these rules, and one draw needn't show every extreme that they name: `front_panel`: its first 512 rows are, in all 512 columns, a symmetric positive definite block. `map_one`: distinct root row blocks. Of the 20 blocks of one index of row (numbers k * 20 to (k + 1) * 20 - 1) at most 8 are named, and exactly 8 for some index of row. `map_two`: as map_one, drawn independently.
All inputs are finite; a program needn't handle non-finite values.
Results may differ from a plain program's by a relative error of at most 0.0003.
Values may be sent and summed in bfloat16 or wider, within the bound.
A program may use at most 192 MiB of HBM per device.

v0:
```python
import jax
import jax.numpy as jnp
from jax import lax
from jax.sharding import PartitionSpec as P

P_SIZE = 256
BLK = 256


def from_root(value, axis, source):
    kept = jnp.where(lax.axis_index(axis) == source, value, 0).astype(value.dtype)
    return lax.psum(kept, axis)


def inverse_factor(block):
    lower = jnp.linalg.cholesky(block)
    identity = jnp.eye(P_SIZE, dtype=jnp.float32)
    return jax.scipy.linalg.solve_triangular(lower, identity, lower=True)


def diagonal_work(top):
    highest = lax.Precision.HIGHEST
    inverse_one = inverse_factor(top[:P_SIZE, :P_SIZE])
    first_top = jnp.dot(
        top[P_SIZE:, :P_SIZE], inverse_one.T, precision=highest, preferred_element_type=jnp.float32
    )
    second_top = top[P_SIZE:, P_SIZE:] - jnp.dot(
        first_top, first_top.T, precision=highest, preferred_element_type=jnp.float32
    )
    inverse_two = inverse_factor(second_top)
    return (inverse_one, first_top, inverse_two)


def panel_rows(panel, inverse_one, first_top, inverse_two):
    highest = lax.Precision.HIGHEST
    first_cols = jnp.dot(
        panel[:, :P_SIZE], inverse_one.T, precision=highest, preferred_element_type=jnp.float32
    )
    second_in = panel[:, P_SIZE:] - jnp.dot(
        first_cols, first_top.T, precision=highest, preferred_element_type=jnp.float32
    )
    second_cols = jnp.dot(
        second_in, inverse_two.T, precision=highest, preferred_element_type=jnp.float32
    )
    return jnp.concatenate([first_cols, second_cols], 1)


def routing(mapping, local_blocks, row_count):
    owner = mapping // local_blocks
    owner_hot = (owner[:, None] == jnp.arange(row_count, dtype=jnp.int32)[None, :]).astype(
        jnp.int32
    )
    rank = jnp.sum(owner_hot * (jnp.cumsum(owner_hot, 0) - 1), 1)
    return (owner, rank, mapping % local_blocks)


def per_device(front_panel, front_slab, child_one, child_two, map_one, map_two):
    rows_dev = front_slab.shape[0]
    slab_width = front_slab.shape[1]
    panel_width = front_panel.shape[1]
    child_blocks = map_one.shape[0]
    child_local = child_one.shape[0]
    row_count = lax.axis_size("row")
    col_count = lax.axis_size("col")
    row_rank = lax.axis_index("row")
    col_rank = lax.axis_index("col")
    piece = slab_width // row_count
    local_blocks = rows_dev // BLK
    capacity = 2 * child_blocks // row_count

    def split_columns(child):
        return child.reshape(child_local, col_count, piece)

    got_one, got_two = (
        lax.all_to_all(split_columns(child_one), "col", split_axis=1, concat_axis=0, tiled=True),
        lax.all_to_all(split_columns(child_two), "col", split_axis=1, concat_axis=0, tiled=True),
    )

    def send_rows(received, mapping):
        owner, rank, target = routing(mapping, local_blocks, row_count)
        slot = owner * capacity + rank
        select = (
            slot[None, :] == jnp.arange(row_count * capacity, dtype=jnp.int32)[:, None]
        ).astype(jnp.bfloat16)
        blocks = received.reshape(child_blocks, BLK * piece)
        packed = jnp.dot(select, blocks, preferred_element_type=jnp.float32).astype(jnp.bfloat16)
        return packed.reshape(row_count * capacity * BLK, piece)

    arrived_one, arrived_two = (
        lax.all_to_all(send_rows(got_one, map_one), "row", split_axis=0, concat_axis=1, tiled=True),
        lax.all_to_all(send_rows(got_two, map_two), "row", split_axis=0, concat_axis=1, tiled=True),
    )

    def place(arrived, mapping):
        owner, rank, target = routing(mapping, local_blocks, row_count)
        mine = (owner == row_rank)[None, :, None]
        at_block = target[None, :, None] == jnp.arange(local_blocks, dtype=jnp.int32)[:, None, None]
        at_slot = rank[None, :, None] == jnp.arange(capacity, dtype=jnp.int32)[None, None, :]
        placing = jnp.sum((at_block & at_slot & mine).astype(jnp.int32), 1).astype(jnp.bfloat16)
        added = jnp.dot(
            placing, arrived.reshape(capacity, BLK * slab_width), preferred_element_type=jnp.float32
        )
        return added.reshape(rows_dev, slab_width)

    assembled = front_slab + place(arrived_one, map_one) + place(arrived_two, map_two)
    gathered = lax.all_gather(front_panel, "col", axis=1, tiled=True)
    top = gathered[: 2 * P_SIZE]
    top = from_root(top, "row", 0)
    inverse_one, first_top, inverse_two = diagonal_work(top)
    factor = panel_rows(gathered, inverse_one, first_top, inverse_two)
    factor_out = lax.dynamic_slice_in_dim(factor, col_rank * panel_width, panel_width, 1)
    global_rows = row_rank * rows_dev + jnp.arange(rows_dev, dtype=jnp.int32)
    masked = factor * (global_rows >= 2 * P_SIZE)[:, None].astype(jnp.float32)
    wanted = (
        2 * P_SIZE
        + col_rank * slab_width
        + jnp.arange(slab_width, dtype=jnp.int32)
        - row_rank * rows_dev
    )
    valid = ((wanted >= 0) & (wanted < rows_dev))[:, None].astype(jnp.float32)
    picked = jnp.take(factor, jnp.clip(wanted, 0, rows_dev - 1), axis=0) * valid
    slab_rows = lax.psum(picked, "row")
    update = jnp.dot(
        masked, slab_rows.T, precision=lax.Precision.HIGHEST, preferred_element_type=jnp.float32
    )
    return (factor_out, assembled - update)


def solution(mesh):
    in_specs = (P("row", "col"), P("row", "col"), P("col", "row"), P("col", "row"), P(), P())
    out_specs = (P("row", "col"), P("row", "col"))
    return jax.shard_map(
        per_device, mesh=mesh, in_specs=in_specs, out_specs=out_specs, check_vma=False
    )
```

profile of v0, /device:TPU:16, one launch (start us, length us, event | category | flops | bytes accessed | tf_op | source)
XLA Modules:
  0.0 494.9 jit_solution(5786572889173300262)
XLA Ops:
  7.9 2.3 copy.39
  10.2 7.3 %all-to-all-start = ((bf16[512,16,64]{0,2,1:T(8,128)(2,1)}), bf16[512,16,64]{0,2,1:T(8,128)(2,1)S(1)}, u32[]{:S(2)}, u32[]{:S(2)}) async-start(bf16[512,16,64]{0,2,1:T(8,128)(2,1)} %bitcast.11), calls=%async_computation | async-start | bytes 2097152 | tf_op jit(solution)/shard_map/all_to_all | solution.py:75
  18.8 19.8 %all-to-all-done = bf16[512,16,64]{0,2,1:T(8,128)(2,1)S(1)} async-done(((bf16[512,16,64]{0,2,1:T(8,128)(2,1)}), bf16[512,16,64]{0,2,1:T(8,128)(2,1)S(1)}, u32[]{:S(2)}, u32[]{:S(2)}) %all-to-all-start) | async-done | bytes 1048608 | tf_op jit(solution)/shard_map/all_to_all | solution.py:75
  38.7 5.9 %all-to-all-start.2 = ((bf16[512,16,64]{0,2,1:T(8,128)(2,1)}), bf16[512,16,64]{0,2,1:T(8,128)(2,1)S(1)}, u32[]{:S(2)}, u32[]{:S(2)}) async-start(bf16[512,16,64]{0,2,1:T(8,128)(2,1)} %bitcast.15), calls=%async_computation.2 | async-start | bytes 2097152 | tf_op jit(solution)/shard_map/all_to_all | solution.py:76
  44.9 2.0 copy.40
  46.9 2.5 reshape.193
  49.4 1.9 convolution_convert_fusion.1
  51.3 5.5 %all_to_all.49 = bf16[8,2048,64]{2,1,0:T(8,128)(2,1)} reshape(bf16[64,16384]{1,0:T(8,128)(2,1)S(1)} %convolution_convert_fusion.1) | data formatting | bytes 4194304 | tf_op jit(solution)/shard_map/all_to_all | solution.py:90
  56.9 4.8 copy.41
  61.7 6.7 %all-to-all-start.1 = ((bf16[8,2048,64]{1,2,0:T(8,128)(2,1)}), bf16[8,2048,64]{1,2,0:T(8,128)(2,1)S(1)}, u32[]{:S(2)}, u32[]{:S(2)}) async-start(bf16[8,2048,64]{1,2,0:T(8,128)(2,1)} %copy.41), calls=%async_computation.1 | async-start | bytes 4194304 | tf_op jit(solution)/shard_map/all_to_all | solution.py:90
  68.8 1.8 copy.44
  70.6 2.9 reshape.197
  73.5 2.0 convolution_convert_fusion
  75.5 6.5 %all_to_all.55 = bf16[8,2048,64]{2,1,0:T(8,128)(2,1)} reshape(bf16[64,16384]{1,0:T(8,128)(2,1)} %convolution_convert_fusion) | data formatting | bytes 4194304 | tf_op jit(solution)/shard_map/all_to_all | solution.py:91
  82.0 4.8 copy.45
  86.8 8.8 %all-to-all-done.1 = bf16[8,2048,64]{1,2,0:T(8,128)(2,1)S(1)} async-done(((bf16[8,2048,64]{1,2,0:T(8,128)(2,1)}), bf16[8,2048,64]{1,2,0:T(8,128)(2,1)S(1)}, u32[]{:S(2)}, u32[]{:S(2)}) %all-to-all-start.1) | async-done | bytes 2097184 | tf_op jit(solution)/shard_map/all_to_all | solution.py:90
  95.6 4.3 all-to-all-start.3
  101.1 4.2 copy.42
  105.4 5.0 %reshape.232 = bf16[1048576]{0:T(1024)(128)(2,1)S(1)} reshape(bf16[2048,8,64]{2,1,0:T(8,128)(2,1)} %copy.42) | data formatting | bytes 4194304
  110.4 2.2 reshape.194
  112.6 7.9 %fusion.38 = f32[20,131072]{1,0:T(8,128)} fusion(bf16[8,131072]{1,0:T(8,128)(2,1)} %reshape.194, s32[20,8]{1,0:T(8,128)S(1)} %convert_reduce_fusion.1), kind=kOutput, calls=%fused_computation.86 | convolution fusion | flops 41943200 | bytes 12583552 | tf_op jit(solution)/shard_map/dot_general | solution.py:100
  120.6 10.5 %reshape.195 = f32[5120,512]{1,0:T(8,128)} reshape(f32[20,131072]{1,0:T(8,128)} %fusion.38) | data formatting | bytes 20971520 | tf_op jit(solution)/shard_map/reshape | solution.py:103
  131.1 5.6 %copy.46 = bf16[2048,8,64]{2,1,0:T(8,128)(2,1)} copy(bf16[2048,8,64]{0,2,1:T(8,128)(2,1)} %bitcast.18) | data formatting | bytes 4194304 | tf_op jit(solution)/shard_map/all_to_all | solution.py:91
  136.7 5.0 %reshape.230 = bf16[1048576]{0:T(1024)(128)(2,1)S(1)} reshape(bf16[2048,8,64]{2,1,0:T(8,128)(2,1)} %copy.46) | data formatting | bytes 4194304
  141.8 2.2 reshape.198
  144.0 2.3 slice_select_fusion
  146.4 7.9 %fusion.36 = f32[20,131072]{1,0:T(8,128)} fusion(bf16[8,131072]{1,0:T(8,128)(2,1)} %reshape.198, s32[20,8]{1,0:T(8,128)S(1)} %convert_reduce_fusion), kind=kOutput, calls=%fused_computation.84 | convolution fusion | flops 41943200 | bytes 12583552 | tf_op jit(solution)/shard_map/dot_general | solution.py:100
  154.3 11.1 %reshape.199 = f32[5120,512]{1,0:T(8,128)} reshape(f32[20,131072]{1,0:T(8,128)} %fusion.36) | data formatting | bytes 20971520 | tf_op jit(solution)/shard_map/reshape | solution.py:103
  165.4 45.3 %all-reduce.4.cloned.1.call-done = f32[512,512]{0,1:T(8,128)} async-done(((f32[512,512]{0,1:T(8,128)}), f32[512,512]{0,1:T(8,128)}) %all-reduce.4.cloned.1.call-update) | async-done | bytes 1048592 | tf_op jit(solution)/shard_map/psum | solution.py:12
  212.8 11.7 %cholesky.130 = f32[128,128]{1,0:T(8,128)S(1)} custom-call(f32[128,128]{1,0:T(8,128)S(1)} %cholesky.194), custom_call_target="Cholesky" | custom-call | tf_op jit(solution)/shard_map/jit(cholesky)/cholesky | solution.py:16
  224.6 9.8 %custom-call.13 = f32[1,128,128]{1,2,0:T(8,128)S(1)} custom-call(f32[1,128,128]{2,1,0:T(8,128)S(1)} %get-tuple-element.51), custom_call_target="InvertDiagBlocksLowerTriangular" | custom-call | tf_op jit(solution)/shard_map/jit(cholesky)/cholesky | solution.py:16
  234.9 11.7 %cholesky.147 = f32[128,128]{1,0:T(8,128)S(1)} custom-call(f32[128,128]{1,0:T(8,128)S(1)} %convolution_subtract_fusion.5), custom_call_target="Cholesky" | custom-call | tf_op jit(solution)/shard_map/jit(cholesky)/cholesky | solution.py:16
  248.6 3.9 while.4
  252.5 19.8 %custom-call.14 = f32[2,128,128]{1,2,0:T(8,128)S(1)} custom-call(f32[2,128,128]{2,1,0:T(8,128)S(1)} %get-tuple-element.18), custom_call_target="InvertDiagBlocksLowerTriangular" | custom-call | tf_op jit(solution)/shard_map/jit(_solve_triangular)/triangular_solve | solution.py:18
  274.5 11.7 %cholesky.164 = f32[128,128]{1,0:T(8,128)S(1)} custom-call(f32[128,128]{1,0:T(8,128)S(1)} %cholesky.197), custom_call_target="Cholesky" | custom-call | tf_op jit(solution)/shard_map/jit(cholesky)/cholesky | solution.py:16
  286.3 9.8 %custom-call.15 = f32[1,128,128]{1,2,0:T(8,128)S(1)} custom-call(f32[1,128,128]{2,1,0:T(8,128)S(1)} %get-tuple-element.47), custom_call_target="InvertDiagBlocksLowerTriangular" | custom-call | tf_op jit(solution)/shard_map/jit(cholesky)/cholesky | solution.py:16
  296.6 11.7 %cholesky.181 = f32[128,128]{1,0:T(8,128)S(1)} custom-call(f32[128,128]{1,0:T(8,128)S(1)} %convolution_subtract_fusion.4), custom_call_target="Cholesky" | custom-call | tf_op jit(solution)/shard_map/jit(cholesky)/cholesky | solution.py:16
  311.1 4.1 while.5
  315.1 19.9 %custom-call.16 = f32[2,128,128]{1,2,0:T(8,128)S(1)} custom-call(f32[2,128,128]{2,1,0:T(8,128)S(1)} %get-tuple-element.19), custom_call_target="InvertDiagBlocksLowerTriangular" | custom-call | tf_op jit(solution)/shard_map/jit(_solve_triangular)/triangular_solve | solution.py:18
  335.9 6.7 %fusion.4 = f32[256,5120]{1,0:T(8,128)S(1)} fusion(f32[5120,512]{0,1:T(8,128)} %all-gather.2.cloned.1.call-done, f32[128,256]{1,0:T(8,128)S(1)} %fusion.26, f32[128,256]{1,0:T(8,128)S(1)} %fusion.19), kind=kOutput, calls=%fused_computation.14 | convolution fusion | flops 4026597376 | bytes 10747904 | tf_op jit(solution)/shard_map/dot_general | solution.py:36
  342.6 9.0 %convolution_subtract_fusion = f32[5120,256]{0,1:T(8,128)S(1)} fusion(f32[256,5120]{1,0:T(8,128)S(1)} %fusion.4, f32[256,256]{1,0:T(8,128)S(1)} %fusion.8, f32[5120,512]{0,1:T(8,128)} %all-gather.2.cloned.1.call-done), kind=kOutput, calls=%fused_computation.13 | convolution fusion | flops 4027842560 | bytes 15990784 | tf_op jit(solution)/shard_map/dot_general | solution.py:39
  351.6 6.5 %fusion.10 = f32[5120,256]{0,1:T(8,128)} fusion(f32[5120,256]{0,1:T(8,128)S(1)} %convolution_subtract_fusion, f32[128,256]{1,0:T(8,128)S(1)} %fusion.22, f32[128,256]{1,0:T(8,128)S(1)} %fusion.17), kind=kOutput, calls=%fused_computation.30 | convolution fusion | flops 4026597376 | bytes 10747904 | tf_op jit(solution)/shard_map/dot_general | solution.py:42
  358.2 9.3 %pad_maximum_fusion = f32[5120,512]{0,1:T(8,128)} fusion(f32[5120,256]{0,1:T(8,128)} %fusion.10, f32[5120,256]{0,1:T(8,128)} %bitcast.92), kind=kLoop, calls=%fused_computation.8 | loop fusion | flops 2621440 | bytes 20971520 | tf_op jit(solution)/shard_map/concatenate | solution.py:45
  367.5 11.4 %copy.47 = f32[5120,512]{1,0:T(8,128)} copy(f32[5120,512]{0,1:T(8,128)} %pad_maximum_fusion) | data formatting | bytes 20971520 | tf_op jit(solution)/shard_map/concatenate | solution.py:45
  378.9 6.2 %gather_fusion = f32[512,512]{1,0:T(8,128)S(1)} fusion(f32[5120,512]{1,0:T(8,128)} %copy.47, s32[1024]{0:T(1024)S(1)} %pad_clamp_fusion), kind=kCustom, calls=%fused_computation | custom fusion | bytes 2099200 | tf_op jit(solution)/shard_map/jit(_take)/gather | solution.py:121
  386.4 2.0 fusion.7
  388.4 59.9 %all-reduce.6.cloned.1.call-done = f32[512,512]{1,0:T(8,128)} async-done(((f32[512,512]{1,0:T(8,128)}), f32[512,512]{1,0:T(8,128)}) %all-reduce.6.cloned.1.call-update) | async-done | bytes 1048592 | tf_op jit(solution)/shard_map/psum | solution.py:122
  448.3 39.6 %add_subtract_fusion = f32[5120,512]{1,0:T(8,128)} fusion(f32[5120,512]{1,0:T(8,128)} %reshape.199, f32[5120,512]{1,0:T(8,128)} %param.10, f32[5120,512]{1,0:T(8,128)} %reshape.195, f32[512,512]{1,0:T(8,128)} %all-reduce.6.cloned.1.call-done, f32[5120]{0:T(1024)S(1)} %fusion.31, f32[5120,256]{0,1:T(8,128)} %fusion.10, f32[5120,256]{0,1:T(8,128)} %bitcast.94), kind=kOutput, calls=%fused_computation.12 | convolution fusion | flops 16119234560 | bytes 53497856 | tf_op jit(solution)/shard_map/dot_general | solution.py:123
  (90 shorter events, 21.5 us)
Async XLA Ops:
  7.2 10.3 %copy-start.3 = (bf16[512,1024]{1,0:T(8,128)(2,1)S(1)}, bf16[512,1024]{1,0:T(8,128)(2,1)}, u32[]{:S(2)}) copy-start(bf16[512,1024]{1,0:T(8,128)(2,1)} %param.12) | copy-start | bytes 3145732
  7.2 37.4 %copy-start.5 = (s32[32]{0:T(128)S(1)}, s32[32]{0:T(128)}, u32[]{:S(2)}) copy-start(s32[32]{0:T(128)} %param.13) | copy-start | bytes 388
  7.2 37.4 %copy-start.4 = (s32[32]{0:T(128)S(1)}, s32[32]{0:T(128)}, u32[]{:S(2)}) copy-start(s32[32]{0:T(128)} %param.14) | copy-start | bytes 388
  7.2 136.8 %all-gather.2.cloned.1.call-start = ((), (), s32[]{:S(2)}) async-start(), calls=%async_computation.4 | async-start | bytes 11141120 | tf_op jit(solution)/shard_map/all_gather | solution.py:106
  10.2 28.5 %all-to-all-start = ((bf16[512,16,64]{0,2,1:T(8,128)(2,1)}), bf16[512,16,64]{0,2,1:T(8,128)(2,1)S(1)}, u32[]{:S(2)}, u32[]{:S(2)}) async-start(bf16[512,16,64]{0,2,1:T(8,128)(2,1)} %bitcast.11), calls=%async_computation | async-start | bytes 2097152 | tf_op jit(solution)/shard_map/all_to_all | solution.py:75
  38.7 6.2 %copy-start.1 = (bf16[512,16,64]{0,2,1:T(8,128)(2,1)}, bf16[512,16,64]{0,2,1:T(8,128)(2,1)S(1)}, u32[]{:S(2)}) copy-start(bf16[512,16,64]{0,2,1:T(8,128)(2,1)S(1)} %all-to-all-done) | copy-start | bytes 3145732
  38.7 23.0 %all-to-all-start.2 = ((bf16[512,16,64]{0,2,1:T(8,128)(2,1)}), bf16[512,16,64]{0,2,1:T(8,128)(2,1)S(1)}, u32[]{:S(2)}, u32[]{:S(2)}) async-start(bf16[512,16,64]{0,2,1:T(8,128)(2,1)} %bitcast.15), calls=%async_computation.2 | async-start | bytes 2097152 | tf_op jit(solution)/shard_map/all_to_all | solution.py:76
  61.7 33.9 %all-to-all-start.1 = ((bf16[8,2048,64]{1,2,0:T(8,128)(2,1)}), bf16[8,2048,64]{1,2,0:T(8,128)(2,1)S(1)}, u32[]{:S(2)}, u32[]{:S(2)}) async-start(bf16[8,2048,64]{1,2,0:T(8,128)(2,1)} %copy.41), calls=%async_computation.1 | async-start | bytes 4194304 | tf_op jit(solution)/shard_map/all_to_all | solution.py:90
  95.6 35.5 %all-to-all-start.3 = ((bf16[8,2048,64]{1,2,0:T(8,128)(2,1)}), bf16[8,2048,64]{1,2,0:T(8,128)(2,1)}, u32[]{:S(2)}, u32[]{:S(2)}) async-start(bf16[8,2048,64]{1,2,0:T(8,128)(2,1)} %copy.45), calls=%async_computation.3 | async-start | bytes 4194304 | tf_op jit(solution)/shard_map/all_to_all | solution.py:91
  100.0 110.7 %all-reduce.4.cloned.1.call-start = ((), (), s32[]{:S(2)}) async-start(), calls=%async_computation.5 | async-start | bytes 2097152 | tf_op jit(solution)/shard_map/psum | solution.py:12
  146.3 302.0 %all-reduce.6.cloned.1.call-start = ((), (), s32[]{:S(2)}) async-start(), calls=%async_computation.6 | async-start | bytes 2097152 | tf_op jit(solution)/shard_map/psum | solution.py:122
  210.6 62.7 %copy-start.2 = (f32[512,512]{0,1:T(8,128)S(1)}, f32[512,512]{0,1:T(8,128)}, u32[]{:S(2)}) copy-start(f32[512,512]{0,1:T(8,128)} %all-reduce.4.cloned.1.call-done) | copy-start | bytes 3145732
  342.6 9.0 %copy-start = (f32[256,5120]{1,0:T(8,128)}, f32[256,5120]{1,0:T(8,128)S(1)}, u32[]{:S(2)}) copy-start(f32[256,5120]{1,0:T(8,128)S(1)} %fusion.4) | copy-start | bytes 15728644
Sparse Core Ops, SparseCore 0:
  10.2 88.1 all-gather.1
  146.4 64.1 all-reduce.3
  386.5 61.7 all-reduce.5
where the time goes:
time: 502 us; the launch traced here: 495 us
  waiting for transfers between devices  135 us (27%)
  other arithmetic  126 us (25%)
  local copies, waits for them, and re-layouts  107 us (21%)
  matrix products  85.3 us (17%)
  starting transfers between devices  24.5 us (5%)
  between operations  17.2 us (3%)
    another operation x13, other arithmetic, inverse_factor(): lower = jnp.linalg.cholesky(block)  68.6 us
    psum x1, waiting for transfers between devices, per_device(): slab_rows = lax.psum(picked, 'row')  59.9 us
    psum x1, waiting for transfers between devices, from_root(): return lax.psum(kept, axis)  45.3 us
    another operation x5, other arithmetic, inverse_factor(): return jax.scipy.linalg.solve_triangular(lower, identity, lower=True)  39.8 us
    dot_general x1, matrix products, per_device(): jnp.dot(masked, slab_rows.T, precision=lax.Precision.HIGHEST, preferred_e...  39.6 us
    reshape x2, local copies, waits for them, and re-layouts, place(): return added.reshape(rows_dev, slab_width)  21.6 us
    all_to_all x1, waiting for transfers between devices, per_device(): lax.all_to_all(split_columns(child_one), 'col', split_axis=1, concat_axis...  19.8 us
    all_to_all x3, local copies, waits for them, and re-layouts, per_device(): lax.all_to_all(send_rows(got_two, map_two), 'row', split_axis=0, concat_a...  16.9 us
  transfers between devices with their start and end apart: 7, of which 4 were waited for; matrix products, arithmetic and copies ran while one was open for 19% of the time, Pallas kernels for 0%

commit v1 on v0

v1 whole, which is shorter than its diff:
```python
import functools

import jax
import jax.numpy as jnp
from jax import lax
from jax.experimental import pallas as pl
from jax.experimental.pallas import tpu as pltpu
from jax.sharding import PartitionSpec as P

BLK = 256
PANEL = 512
NC = 16
NR = 8
STRIP = 32
ROWS = 5120
HALF = ROWS // 2
WIDTH = 512
CAP = 8
NS = 2
SUB = BLK // NS
MESH = pl.DeviceIdType.MESH
F32 = jnp.float32
BF16 = jnp.bfloat16
HIGHEST = lax.Precision.HIGHEST


def swap_halves(v):
    return jnp.concatenate([v[:, 64:], v[:, :64]], axis=1)


def exchange_kernel(
    slots, panel, child_one, child_two,
    top, rows_ps, code, scale, arrived,
    pack, got, blocks, outgoing, coded, scales,
    top_send, top_recv, topz_recv, c1_send, c1_recv, c2_send, c2_recv,
    g_send, g_recv, s_send, s_recv, ps_send, ps_recv, psb_send, psb_recv,
):
    row = lax.axis_index("row")
    col = lax.axis_index("col")
    z, core = row // 2, row % 2
    x, y = col // 4, col % 4
    other = z * 2 + (1 - core)

    def at_col(dx, dy):
        return ((x + dx) % 4) * 4 + (y + dy) % 4

    def at_row(dz, dk):
        return ((z + dz) % 4) * 2 + (core + dk) % 2

    plane = [(dx, dy) for dx in range(4) for dy in range(4)]
    away = [d for d in plane if d != (0, 0)]
    line = [(dz, dk) for dz in range(4) for dk in range(2)]
    line_away = [d for d in line if d != (0, 0)]

    barrier = pltpu.get_barrier_semaphore()
    for d in away:
        pl.semaphore_signal(barrier, inc=1, device_id=(row, at_col(*d)), device_id_type=MESH)
    for d in plane:
        pl.semaphore_signal(barrier, inc=1, device_id=(other, at_col(*d)), device_id_type=MESH)
    for dz in range(1, 4):
        for dk in range(2):
            pl.semaphore_signal(barrier, inc=1, device_id=(at_row(dz, dk), col), device_id_type=MESH)
    pl.semaphore_wait(barrier, 37)

    sends = []

    def remote(src, dst, send, recv, to_row, to_col):
        return pltpu.make_async_remote_copy(
            src_ref=src, dst_ref=dst, send_sem=send, recv_sem=recv,
            device_id=(to_row, to_col), device_id_type=MESH,
        )

    def push(*args):
        copy = remote(*args)
        copy.start()
        sends.append(copy)

    def landed(ref, sem):
        pltpu.make_async_copy(ref, ref, sem).wait()

    mine = pl.ds(pl.multiple_of(col * STRIP, STRIP), STRIP)
    strip = panel.at[:, pl.ds(0, PANEL)]

    @pl.when(row == 0)
    def _():
        for n, d in enumerate(line_away):
            remote(strip, top.at[mine], top_send.at[n], topz_recv, at_row(*d), col).start()
        pltpu.make_async_copy(strip, top.at[mine], topz_recv).start()

    landed(top.at[mine], topz_recv)
    for n, d in enumerate(away):
        push(top.at[mine], top.at[mine], top_send.at[7 + n], top_recv.at[col], row, at_col(*d))

    low = lax.broadcasted_iota(jnp.int32, (SUB, 128), 1) < 64
    for s in range(NS):
        for t, child in enumerate((child_one, child_two)):
            for p in range(NC // 2):
                lanes = slice(128 * p, 128 * p + 128)
                first = child[s * SUB:(s + 1) * SUB, lanes]
                second = child[BLK + s * SUB:BLK + (s + 1) * SUB, lanes]
                pack[s, t, 2 * p] = jnp.where(low, first, swap_halves(second))
                pack[s, t, 2 * p + 1] = jnp.where(low, swap_halves(first), second)
        for n, d in enumerate(plane):
            for dk in range(2):
                to = (core + dk) % 2
                src = pack.at[s, to, at_col(*d)]
                dst = got.at[s, col, core]
                if d == (0, 0) and dk == 0:
                    pltpu.make_async_copy(src, dst, c1_recv.at[s, col, core]).start()
                else:
                    push(src, dst, c1_send.at[s, n, dk], c1_recv.at[s, col, core], z * 2 + to, at_col(*d))

    for v in range(9):
        for g in range(2):
            if v + 9 * g < NC:
                to_col = v + 9 * g
                src = panel.at[:, pl.ds(PANEL * (v + 1 - g), PANEL)]

                @pl.when((row == g) & (col != to_col))
                def _():
                    remote(src, rows_ps.at[mine], ps_send.at[v], ps_recv.at[col], row, to_col).start()

                @pl.when((row == g) & (col == to_col))
                def _():
                    pltpu.make_async_copy(src, rows_ps.at[mine], ps_recv.at[col]).start()

    for j in range(ROWS // 128):
        lanes = slice(128 * j, 128 * j + 128)
        v = panel[:, lanes]
        most = jnp.maximum(jnp.max(jnp.abs(v), axis=0, keepdims=True), 1e-30)
        step = most * (1.0 / 32760.0)
        coded[:, lanes] = jnp.round(v * (1.0 / step)).astype(jnp.int32).astype(jnp.int16)
        scales[j:j + 1, :] = step
    pltpu.make_async_copy(scales, scale.at[col], s_recv.at[col]).start()
    for n, d in enumerate(away):
        push(scales, scale.at[col], s_send.at[n], s_recv.at[col], row, at_col(*d))
    halves = [pl.ds(0, HALF), pl.ds(HALF, HALF)]
    for h in range(2):
        pltpu.make_async_copy(coded.at[:, halves[h]], code.at[mine, halves[h]], g_recv.at[h, col]).start()
        for n in range(1, 4):
            d = (n, 0) if h == 0 else (0, n)
            push(coded.at[:, halves[h]], code.at[mine, halves[h]], g_send.at[h, n - 1], g_recv.at[h, col], row, at_col(*d))

    def second_hop(n):
        for h in range(2):
            d = (n, 0) if h == 0 else (0, n)
            source = at_col(*d)
            part = code.at[pl.ds(pl.multiple_of(source * STRIP, STRIP), STRIP), halves[h]]
            landed(part, g_recv.at[h, source])
            for m in range(1, 4):
                to = at_col(0, m) if h == 0 else at_col(m, 0)
                push(part, part, g_send.at[h, 3 + 3 * n + m - 1], g_recv.at[h, source], row, to)

    def rows_hop(s):
        for d in plane:
            for dk in range(2):
                source, k = at_col(*d), (core + dk) % 2
                landed(got.at[s, source, k], c1_recv.at[s, source, k])
        for c in range(NC):
            first = got[s, c, 0]
            second = got[s, c, 1]
            blocks[s, 2 * c] = jnp.where(low, first, swap_halves(second))
            blocks[s, 2 * c + 1] = jnp.where(low, swap_halves(first), second)
        for n, d in enumerate(line):
            to = at_row(*d)
            for q in range(CAP):
                outgoing[s, to, q] = blocks[s, slots[core * NR * CAP + to * CAP + q]]
            dst = arrived.at[core, z, s]
            if d == (0, 0):
                pltpu.make_async_copy(outgoing.at[s, to], dst, c2_recv.at[s, z, core]).start()
            else:
                push(outgoing.at[s, to], dst, c2_send.at[s, n], c2_recv.at[s, z, core], to, col)

    rows_hop(0)
    for n in range(4):
        second_hop(n)
    rows_hop(1)

    root = jnp.where(col < 9, 0, 1)

    @pl.when(row == root)
    def _():
        for d in plane:
            source = at_col(*d)
            landed(rows_ps.at[pl.ds(pl.multiple_of(source * STRIP, STRIP), STRIP)], ps_recv.at[source])
        for n, d in enumerate(((1, 0), (3, 0), (2, 0), (0, 1))):
            remote(rows_ps, rows_ps, psb_send.at[n], psb_recv, at_row(*d), col).start()
        for n, d in enumerate(((1, 0), (3, 0), (2, 0), (0, 1))):
            remote(rows_ps, rows_ps, psb_send.at[n], psb_recv, at_row(*d), col).wait_send()

    @pl.when(row != root)
    def _():
        landed(rows_ps, psb_recv)

    @pl.when((core == root) & (z > 0))
    def _():
        remote(rows_ps, rows_ps, psb_send.at[3], psb_recv, other, col).start()
        remote(rows_ps, rows_ps, psb_send.at[3], psb_recv, other, col).wait_send()

    @pl.when(row == 0)
    def _():
        for n, d in enumerate(line_away):
            remote(strip, top.at[mine], top_send.at[n], topz_recv, at_row(*d), col).wait_send()

    for v in range(9):
        for g in range(2):
            if v + 9 * g < NC:
                to_col = v + 9 * g
                src = panel.at[:, pl.ds(PANEL * (v + 1 - g), PANEL)]

                @pl.when((row == g) & (col != to_col))
                def _():
                    remote(src, rows_ps.at[mine], ps_send.at[v], ps_recv.at[col], row, to_col).wait_send()

    for d in away:
        source = at_col(*d)
        where = pl.ds(pl.multiple_of(source * STRIP, STRIP), STRIP)
        landed(top.at[where], top_recv.at[source])
        landed(scale.at[source], s_recv.at[source])
        if d[1] != 0:
            landed(code.at[where, halves[0]], g_recv.at[0, source])
        if d[0] != 0:
            landed(code.at[where, halves[1]], g_recv.at[1, source])
    landed(scale.at[col], s_recv.at[col])
    for s in range(NS):
        for dz, dk in line:
            k, from_z = (core + dk) % 2, (z + dz) % 4
            landed(arrived.at[k, from_z, s], c2_recv.at[s, from_z, k])
    for copy in sends:
        copy.wait_send()


def exchange(slots, panel, child_one, child_two):
    vmem = pl.BlockSpec(memory_space=pltpu.VMEM)
    anywhere = pl.BlockSpec(memory_space=pl.ANY)
    dma = pltpu.SemaphoreType.DMA
    return pl.pallas_call(
        exchange_kernel,
        out_shape=(
            jax.ShapeDtypeStruct((PANEL, PANEL), F32),
            jax.ShapeDtypeStruct((PANEL, WIDTH), F32),
            jax.ShapeDtypeStruct((PANEL, ROWS), jnp.int16),
            jax.ShapeDtypeStruct((NC, ROWS // 128, 128), F32),
            jax.ShapeDtypeStruct((2, 4, NS, CAP, SUB, 128), BF16),
        ),
        in_specs=[pl.BlockSpec(memory_space=pltpu.SMEM), vmem, vmem, vmem],
        out_specs=(vmem, vmem, anywhere, anywhere, anywhere),
        scratch_shapes=[
            pltpu.VMEM((NS, 2, NC, SUB, 128), BF16),
            pltpu.VMEM((NS, NC, 2, SUB, 128), BF16),
            pltpu.VMEM((NS, 2 * NC, SUB, 128), BF16),
            pltpu.VMEM((NS, NR, CAP, SUB, 128), BF16),
            pltpu.VMEM((STRIP, ROWS), jnp.int16),
            pltpu.VMEM((ROWS // 128, 128), F32),
            dma((22,)), dma((NC,)), dma(()),
            dma((NS, NC, 2)), dma((NS, NC, 2)),
            dma((NS, NR)), dma((NS, 4, 2)),
            dma((2, 15)), dma((2, NC)),
            dma((15,)), dma((NC,)),
            dma((9,)), dma((NC,)),
            dma((4,)), dma(()),
        ],
        compiler_params=pltpu.CompilerParams(
            collective_id=0, has_side_effects=True, vmem_limit_bytes=48 * 1024 * 1024
        ),
    )(slots, panel, child_one, child_two)


def eliminate(block):
    lane = lax.broadcasted_iota(jnp.int32, (8, 128), 1)
    sub = lax.broadcasted_iota(jnp.int32, (8, 128), 0)
    v = [block[8 * h:8 * h + 8, :] for h in range(16)]
    for j in range(128):
        g, jj = j // 8, j % 8
        here = lane == j
        column = jnp.broadcast_to(v[g][:, j:j + 1], (8, 128))
        pivot = jnp.broadcast_to(column[jj:jj + 1, :], (8, 128))
        line = jnp.broadcast_to(v[g][jj:jj + 1, :], (8, 128))
        root = lax.rsqrt(pivot)
        inverse = root * root
        scaled = jnp.where(here, 1.0, line) * inverse
        below = sub > jj
        for h in range(g + 1, 16):
            factor = jnp.broadcast_to(v[h][:, j:j + 1], (8, 128))
            v[h] = jnp.where(here, 0.0, v[h]) - factor * scaled
        v[g] = jnp.where(
            below,
            jnp.where(here, 0.0, v[g]) - column * scaled,
            jnp.where(sub == jj, jnp.where(here, 1.0, v[g]) * root, v[g]),
        )
    return [jnp.where(lane <= 8 * h + sub, v[h], 0.0) for h in range(16)]


def solve_kernel(top, rows_ps, w_high, w_low, own_high, own_low, work, inverse):
    work[...] = top[...]
    blk = lax.broadcasted_iota(jnp.int32, (PANEL, PANEL), 1) // 128
    eye = (
        lax.broadcasted_iota(jnp.int32, (128, PANEL), 0)
        == lax.broadcasted_iota(jnp.int32, (128, PANEL), 1) % 128
    ).astype(F32)
    for k in range(4):
        rows = slice(128 * k, 128 * k + 128)
        for h, part in enumerate(eliminate(work[rows, rows])):
            inverse[8 * h:8 * h + 8, :] = part
        line = jnp.where(blk[:128] == k, eye, work[rows, :])
        done = jnp.dot(inverse[...], line, precision=HIGHEST, preferred_element_type=F32)
        work[rows, :] = done
        if k < 3:
            rest = slice(128 * k + 128, PANEL)
            count = PANEL - 128 * k - 128
            work[rest, :] = jnp.where(blk[:count] == k, 0.0, work[rest, :]) - lax.dot_general(
                done[:, rest], done, (((0,), (0,)), ((), ())),
                precision=HIGHEST, preferred_element_type=F32,
            )
    lower = lax.broadcasted_iota(jnp.int32, (PANEL, PANEL), 0) >= lax.broadcasted_iota(jnp.int32, (PANEL, PANEL), 1)
    work[...] = jnp.where(lower, work[...], 0.0)
    half = jnp.dot(work[...], rows_ps[...], precision=HIGHEST, preferred_element_type=F32)
    w = lax.dot_general(
        work[...], half, (((0,), (0,)), ((), ())), precision=HIGHEST, preferred_element_type=F32
    )
    high = w.astype(BF16)
    w_high[...] = high
    w_low[...] = (w - high.astype(F32)).astype(BF16)
    col = lax.axis_index("col")
    own = work[pl.ds(pl.multiple_of(col * STRIP, STRIP), STRIP), :]
    high = own.astype(BF16)
    own_high[...] = high
    own_low[...] = (own - high.astype(F32)).astype(BF16)


def solve(top, rows_ps):
    vmem = pl.BlockSpec(memory_space=pltpu.VMEM)
    return pl.pallas_call(
        solve_kernel,
        out_shape=(
            jax.ShapeDtypeStruct((PANEL, WIDTH), BF16),
            jax.ShapeDtypeStruct((PANEL, WIDTH), BF16),
            jax.ShapeDtypeStruct((STRIP, PANEL), BF16),
            jax.ShapeDtypeStruct((STRIP, PANEL), BF16),
        ),
        in_specs=[vmem, vmem],
        out_specs=(vmem,) * 4,
        scratch_shapes=[pltpu.VMEM((PANEL, PANEL), F32), pltpu.VMEM((128, 128), F32)],
        compiler_params=pltpu.CompilerParams(vmem_limit_bytes=40 * 1024 * 1024),
    )(top, rows_ps)


def update_kernel(
    where, has, slab, code, scale, first, second, w_high, w_low, own_high, own_low,
    out, factor, high_ref, low_ref,
):
    i = pl.program_id(0)
    row = lax.axis_index("row")
    for c in range(NC):
        part = slice(STRIP * c, STRIP * c + STRIP)
        for half in range(2):
            lanes = slice(128 * half, 128 * half + 128)
            step = scale[c, pl.ds(2 * i + half, 1), :]
            v = code[part, lanes].astype(jnp.int32).astype(F32) * step
            high = v.astype(BF16)
            high_ref[part, lanes] = high
            low_ref[part, lanes] = (v - high.astype(F32)).astype(BF16)
    high, low = high_ref[...], low_ref[...]

    def left(a, b):
        return lax.dot_general(a, b, (((0,), (0,)), ((), ())), preferred_element_type=F32)

    def right(a, b):
        return jnp.dot(a, b, preferred_element_type=F32)

    factor[...] = (
        right(own_high[...], high) + right(own_high[...], low) + right(own_low[...], high)
    )
    update = left(high, w_high[...]) + left(low, w_high[...]) + left(high, w_low[...])
    keep = (row * (ROWS // BLK) + i) >= PANEL // BLK
    update = jnp.where(keep, update, 0.0)
    for s in range(NS):
        rows = slice(SUB * s, SUB * s + SUB)
        for a in range(4):
            lanes = slice(128 * a, 128 * a + 128)
            one = jnp.where(has[i] > 0, first[0, a, s, 0].astype(F32), 0.0)
            two = jnp.where(has[ROWS // BLK + i] > 0, second[0, a, s, 0].astype(F32), 0.0)
            out[rows, lanes] = ((slab[rows, lanes] + one) + two) - update[rows, lanes]


def update(where, has, slab, code, scale, arrived, w_high, w_low, own_high, own_low):
    steps = ROWS // BLK

    def whole(shape):
        return pl.BlockSpec(shape, lambda i, w, h: (0,) * len(shape))

    def child(t):
        return pl.BlockSpec(
            (1, 4, NS, 1, SUB, 128), lambda i, w, h: (t, 0, 0, w[t * steps + i], 0, 0)
        )

    return pl.pallas_call(
        update_kernel,
        grid_spec=pltpu.PrefetchScalarGridSpec(
            num_scalar_prefetch=2,
            grid=(steps,),
            in_specs=[
                pl.BlockSpec((BLK, WIDTH), lambda i, w, h: (i, 0)),
                pl.BlockSpec((PANEL, BLK), lambda i, w, h: (0, i)),
                whole((NC, ROWS // 128, 128)),
                child(0),
                child(1),
                whole((PANEL, WIDTH)),
                whole((PANEL, WIDTH)),
                whole((STRIP, PANEL)),
                whole((STRIP, PANEL)),
            ],
            out_specs=[
                pl.BlockSpec((BLK, WIDTH), lambda i, w, h: (i, 0)),
                pl.BlockSpec((STRIP, BLK), lambda i, w, h: (0, i)),
            ],
            scratch_shapes=[pltpu.VMEM((PANEL, BLK), BF16), pltpu.VMEM((PANEL, BLK), BF16)],
        ),
        out_shape=(
            jax.ShapeDtypeStruct((ROWS, WIDTH), F32),
            jax.ShapeDtypeStruct((STRIP, ROWS), F32),
        ),
        compiler_params=pltpu.CompilerParams(vmem_limit_bytes=40 * 1024 * 1024),
    )(where, has, slab, code, scale, arrived, arrived, w_high, w_low, own_high, own_low)


def routing(maps):
    steps = ROWS // BLK
    owner = maps // steps
    count = maps.shape[1]
    before = jnp.arange(count)[None, :] < jnp.arange(count)[:, None]
    same = owner[:, :, None] == owner[:, None, :]
    rank = jnp.sum((same & before[None]).astype(jnp.int32), 2)
    slot = owner * CAP + rank
    hit = slot[:, None, :] == jnp.arange(NR * CAP)[None, :, None]
    slots = jnp.sum(jnp.where(hit, jnp.arange(count)[None, None, :], 0), 2)
    mine = lax.axis_index("row") * steps + jnp.arange(steps)
    at = maps[:, None, :] == mine[None, :, None]
    where = jnp.sum(jnp.where(at, rank[:, None, :], 0), 2)
    has = jnp.sum(at.astype(jnp.int32), 2)
    return tuple(v.reshape(-1).astype(jnp.int32) for v in (slots, where, has))


def per_device(front_panel, front_slab, child_one, child_two, map_one, map_two):
    slots, where, has = routing(jnp.stack([map_one, map_two]))
    top, rows_ps, code, scale, arrived = exchange(slots, front_panel.T, child_one, child_two)
    parts = solve(top, rows_ps)
    slab, factor = update(where, has, front_slab, code, scale, arrived, *parts)
    return (factor.T, slab)


def solution(mesh):
    in_specs = (P("row", "col"), P("row", "col"), P("col", "row"), P("col", "row"), P(), P())
    out_specs = (P("row", "col"), P("row", "col"))
    return jax.shard_map(
        per_device, mesh=mesh, in_specs=in_specs, out_specs=out_specs, check_vma=False
    )
```

time: 502 us -> 228 us (0.45)
  Pallas kernels: 0 us -> 213 us
  waiting for transfers between devices: 135 us -> 0 us
  other arithmetic: 126 us -> 1.81 us
  local copies, waits for them, and re-layouts: 107 us -> 8.64 us
  matrix products: 85.3 us -> 0 us
  starting transfers between devices: 24.5 us -> 0 us
  between operations: 17.2 us -> 0.69 us
    pallas_call x0 -> x3, Pallas kernels: none -> 213 us  [the longest x1 114 us: exchange(): pl.pallas_call(exchange_kernel, out_shape=(jax.ShapeDtypeStruct((PANEL, P...]
    another operation x20 -> x0, other arithmetic: 109 us -> none  [the longest x13 68.6 us: inverse_factor(): lower = jnp.linalg.cholesky(block)]
    psum x2 -> x0, waiting for transfers between devices: 105 us -> none  [the longest x1 59.9 us: per_device(): slab_rows = lax.psum(picked, 'row')]
    dot_general x10 -> x0, matrix products: 82.6 us -> none  [the longest x1 39.6 us: per_device(): jnp.dot(masked, slab_rows.T, precision=lax.Precision.HIGHEST, preferred_e...]
    all_to_all x8 -> x0, local copies, waits for them, and re-layouts: 35.3 us -> none  [the longest x3 16.9 us: per_device(): lax.all_to_all(send_rows(got_two, map_two), 'row', split_axis=0, concat_a...]
    reshape x6 -> x3, local copies, waits for them, and re-layouts: 31.4 us -> 0.25 us  [routing(): return tuple((v.reshape(-1).astype(jnp.int32) for v in (slots, where, has)))]
    all_to_all x4 -> x0, waiting for transfers between devices: 28.6 us -> none  [the longest x1 19.8 us: per_device(): lax.all_to_all(split_columns(child_one), 'col', split_axis=1, concat_axis...]
    all_to_all x4 -> x0, starting transfers between devices: 24.2 us -> none  [the longest x1 7.28 us: per_device(): lax.all_to_all(split_columns(child_one), 'col', split_axis=1, concat_axis...]
  transfers between devices with their start and end apart: 7 -> 0, of which waited for: 4 -> 0; matrix products, arithmetic and copies ran while one was open for 19% -> 0% of each run, Pallas kernels for 0% -> 0%
where the time goes in v1:
time: 228 us; the launch traced here: 224 us
  Pallas kernels  213 us (93%)
  local copies, waits for them, and re-layouts  8.64 us (4%)
    pallas_call x1, Pallas kernels, exchange(): pl.pallas_call(exchange_kernel, out_shape=(jax.ShapeDtypeStruct((PANEL, P...  114 us
    pallas_call x1, Pallas kernels, solve(): pl.pallas_call(solve_kernel, out_shape=(jax.ShapeDtypeStruct((PANEL, WIDT...  75.5 us
    pallas_call x1, Pallas kernels, update(): pl.pallas_call(update_kernel, grid_spec=pltpu.PrefetchScalarGridSpec(num_...  22.9 us
    unnamed x10, local copies, waits for them, and re-layouts  8.21 us

profile of v1, /device:TPU:16, one launch (start us, length us, event | category | flops | bytes accessed | tf_op | source)
XLA Modules:
  0.0 223.8 jit_solution(4674753187059123900)
XLA Ops:
  0.6 0.7 and_select_fusion
  1.4 0.2 convert_reduce_fusion
  1.5 0.1 select_reduce_fusion
  1.6 0.1 reshape.161.slots
  1.7 0.8 fusion.1
  2.5 0.1 copy.9
  2.6 0.1 reshape.160.has
  2.7 0.1 copy.8
  2.8 0.1 reshape.159.where
  2.9 0.0 copy-start.2
  2.9 1.2 copy-done.2
  4.1 0.0 copy-start.3
  4.1 1.2 copy-done.3
  5.3 0.0 copy-start.4
  5.4 1.1 copy-done.4
  6.4 114.3 %shard_map.77 = (f32[512,512]{1,0:T(8,128)S(1)}, f32[512,512]{1,0:T(8,128)S(1)}, s16[512,5120]{1,0:T(8,128)(2,1)}, f32[16,40,128]{2,1,0:T(8,128)S(1)}, bf16[2,4,2,8,128,128]{5,4,3,2,1,0:T(8,128)(2,1)}) custom-call(s32[128]{0:T(128)S(1)} %reshape.161.slots, f32[32,5120]{1,0:T(8,128)S(1)} %bitcast.4, bf16[512,1024]{1,0:T(8,128)(2,1)S(1)} %copy-done.2, ...), custom_call_target="tpu_custom_call" | custom-call | tf_op jit(solution)/shard_map/pallas_call | solution.py:237
  120.7 75.5 %shard_map.78 = (bf16[512,512]{1,0:T(8,128)(2,1)S(1)}, bf16[512,512]{1,0:T(8,128)(2,1)S(1)}, bf16[32,512]{1,0:T(8,128)(2,1)S(1)}, bf16[32,512]{1,0:T(8,128)(2,1)S(1)}) custom-call(f32[512,512]{1,0:T(8,128)S(1)} %get-tuple-element.16.top, f32[512,512]{1,0:T(8,128)S(1)} %get-tuple-element.17.rows_ps), custom_call_target="tpu_custom_call" | custom-call | tf_op jit(solution)/shard_map/pallas_call | solution.py:333
  196.3 0.0 copy-start
  196.3 2.2 copy-done
  198.4 0.0 copy-start.1
  198.4 2.5 %copy-done.1 = s16[512,5120]{1,0:T(8,128)(2,1)S(1)} copy-done((s16[512,5120]{1,0:T(8,128)(2,1)S(1)}, s16[512,5120]{1,0:T(8,128)(2,1)}, u32[]{:S(2)}) %copy-start.1) | copy-done | bytes 5242904
  200.9 22.9 %shard_map.79 = (f32[5120,512]{1,0:T(8,128)}, f32[32,5120]{1,0:T(8,128)}) custom-call(s32[40]{0:T(128)S(1)} %reshape.159.where, s32[40]{0:T(128)S(1)} %reshape.160.has, f32[5120,512]{1,0:T(8,128)} %slab.1, s16[512,5120]{1,0:T(8,128)(2,1)S(1)} %copy-done.1, f32[16,40,128]{2,1,0:T(8,128)S(1)} %get-tuple-element.14.scale, ...), custom_call_target="tpu_custom_call" | custom-call | tf_op jit(solution)/shard_map/pallas_call | solution.py:397
  (3 shorter events, 0.0 us)
Async XLA Ops:
  2.9 1.2 copy-start.2
  4.1 1.2 copy-start.3
  5.3 1.1 copy-start.4
  196.3 2.2 copy-start
  198.4 2.5 %copy-start.1 = (s16[512,5120]{1,0:T(8,128)(2,1)S(1)}, s16[512,5120]{1,0:T(8,128)(2,1)}, u32[]{:S(2)}) copy-start(s16[512,5120]{1,0:T(8,128)(2,1)} %get-tuple-element.13.code) | copy-start | bytes 15728644

commit v2 on v1

v2 whole, which is shorter than its diff:
```python
import functools

import jax
import jax.numpy as jnp
from jax import lax
from jax.experimental import pallas as pl
from jax.experimental.pallas import tpu as pltpu
from jax.sharding import PartitionSpec as P

BLK = 256
PANEL = 512
NC = 16
NR = 8
STRIP = 32
ROWS = 5120
HALF = ROWS // 2
WIDTH = 512
CAP = 8
NS = 2
SUB = BLK // NS
MESH = pl.DeviceIdType.MESH
F32 = jnp.float32
BF16 = jnp.bfloat16
HIGHEST = lax.Precision.HIGHEST


def swap_halves(v):
    return jnp.concatenate([v[:, 64:], v[:, :64]], axis=1)


def eliminate(block):
    lane = lax.broadcasted_iota(jnp.int32, (8, 128), 1)
    sub = lax.broadcasted_iota(jnp.int32, (8, 128), 0)
    v = [block[8 * h:8 * h + 8, :] for h in range(16)]

    def spread(h, j):
        return jnp.broadcast_to(v[h][:, j:j + 1], (8, 128))

    def line(tile, r):
        return jnp.broadcast_to(tile[r:r + 1, :], (8, 128))

    for g in range(16):
        base = 8 * g
        inside = (lane >= base) & (lane < base + 8)
        columns = [spread(g, base + i) for i in range(8)]
        a = {(r, i): line(columns[i], r) for i in range(8) for r in range(i, 8)}
        lines = [jnp.where(inside, (lane == base + r).astype(F32), line(v[g], r)) for r in range(8)]
        rest = {h: [spread(h, base + i) for i in range(8)] for h in range(g + 1, 16)}
        for h in range(g + 1, 16):
            v[h] = jnp.where(inside, 0.0, v[h])
        for j in range(8):
            root = lax.rsqrt(a[j, j])
            for i in range(j + 1, 8):
                a[i, j] = a[i, j] * root
            for k in range(j + 1, 8):
                for i in range(k, 8):
                    a[i, k] = a[i, k] - a[i, j] * a[k, j]
            lines[j] = lines[j] * root
            for r in range(j + 1, 8):
                lines[r] = lines[r] - a[r, j] * lines[j]
            for h in range(g + 1, 16):
                f = rest[h][j] * root
                for i in range(j + 1, 8):
                    rest[h][i] = rest[h][i] - a[i, j] * f
                v[h] = v[h] - f * lines[j]
        out = lines[0]
        for r in range(1, 8):
            out = jnp.where(sub == r, lines[r], out)
        v[g] = out
    return [jnp.where(lane <= 8 * h + sub, v[h], 0.0) for h in range(16)]


def halve(v):
    high = v.astype(BF16)
    return high, (v - high.astype(F32)).astype(BF16)


def exchange_kernel(
    slots, panel, child_one, child_two, slab_hbm,
    code, scale, arrived, slab, w_high, w_low, own_high, own_low,
    pack, got, blocks, outgoing, coded, scales, ps_scales,
    top, ps_code, ps_scale, work, inverse, rows_ps,
    load, top_send, topz_recv, top_recv, topx_recv, c1_send, c1_recv, c2_send, c2_recv,
    g_send, g_recv, g3_recv, s_send, s_recv, ps_send, ps_recv, psb_send, psb_recv,
):
    row = lax.axis_index("row")
    col = lax.axis_index("col")
    z, core = row // 2, row % 2
    x, y = col // 4, col % 4
    other = z * 2 + (1 - core)

    def at_col(dx, dy):
        return ((x + dx) % 4) * 4 + (y + dy) % 4

    def at_row(dz, dk):
        return ((z + dz) % 4) * 2 + (core + dk) % 2

    def strip_of(source):
        return pl.ds(pl.multiple_of(source * STRIP, STRIP), STRIP)

    plane = [(dx, dy) for dx in range(4) for dy in range(4)]
    away = [d for d in plane if d != (0, 0)]
    line = [(dz, dk) for dz in range(4) for dk in range(2)]
    line_away = [d for d in line if d != (0, 0)]
    mine = strip_of(col)

    slab_load = pltpu.make_async_copy(slab_hbm, slab, load)

    barrier = pltpu.get_barrier_semaphore()
    for d in away:
        pl.semaphore_signal(barrier, inc=1, device_id=(row, at_col(*d)), device_id_type=MESH)
    for d in plane:
        pl.semaphore_signal(barrier, inc=1, device_id=(other, at_col(*d)), device_id_type=MESH)
    for dz in range(1, 4):
        for dk in range(2):
            pl.semaphore_signal(barrier, inc=1, device_id=(at_row(dz, dk), col), device_id_type=MESH)
    pl.semaphore_wait(barrier, 37)

    sends = []

    def remote(src, dst, send, recv, to_row, to_col):
        return pltpu.make_async_remote_copy(
            src_ref=src, dst_ref=dst, send_sem=send, recv_sem=recv,
            device_id=(to_row, to_col), device_id_type=MESH,
        )

    def push(*args):
        copy = remote(*args)
        copy.start()
        sends.append(copy)

    def landed(ref, sem):
        pltpu.make_async_copy(ref, ref, sem).wait()

    def top_half(k):
        return pl.ds(pl.multiple_of(k * 256, 256), 256)

    def top_out(n, d):
        lanes = pl.ds(256 * d[1], 256)
        return remote(panel.at[:, lanes], top.at[mine, lanes], top_send.at[n], topz_recv, at_row(*d), col)

    @pl.when(row == 0)
    def _():
        for n, d in enumerate(line_away):
            top_out(n, d).start()
        pltpu.make_async_copy(panel.at[:, pl.ds(0, 256)], top.at[mine, pl.ds(0, 256)], topz_recv).start()

    low = lax.broadcasted_iota(jnp.int32, (SUB, 128), 1) < 64

    def columns_hop(s):
        for t, child in enumerate((child_one, child_two)):
            for p in range(NC // 2):
                lanes = slice(128 * p, 128 * p + 128)
                first = child[s * SUB:(s + 1) * SUB, lanes]
                second = child[BLK + s * SUB:BLK + (s + 1) * SUB, lanes]
                pack[s, t, 2 * p] = jnp.where(low, first, swap_halves(second))
                pack[s, t, 2 * p + 1] = jnp.where(low, swap_halves(first), second)
        for n, d in enumerate(plane):
            for dk in range(2):
                to = (core + dk) % 2
                src = pack.at[s, to, at_col(*d)]
                dst = got.at[s, col, core]
                if d == (0, 0) and dk == 0:
                    pltpu.make_async_copy(src, dst, c1_recv.at[s, col, core]).start()
                else:
                    push(src, dst, c1_send.at[s, n, dk], c1_recv.at[s, col, core], z * 2 + to, at_col(*d))

    def rows_hop(s):
        for d in plane:
            for dk in range(2):
                source, k = at_col(*d), (core + dk) % 2
                landed(got.at[s, source, k], c1_recv.at[s, source, k])
        for c in range(NC):
            first = got[s, c, 0]
            second = got[s, c, 1]
            blocks[s, 2 * c] = jnp.where(low, first, swap_halves(second))
            blocks[s, 2 * c + 1] = jnp.where(low, swap_halves(first), second)
        for n, d in enumerate(line):
            to = at_row(*d)
            for q in range(CAP):
                outgoing[s, to, q] = blocks[s, slots[core * NR * CAP + to * CAP + q]]
            dst = arrived.at[core, z, s]
            if d == (0, 0):
                pltpu.make_async_copy(outgoing.at[s, to], dst, c2_recv.at[s, z, core]).start()
            else:
                push(outgoing.at[s, to], dst, c2_send.at[s, n], c2_recv.at[s, z, core], to, col)

    def top_hop():
        lanes = top_half(core)
        landed(top.at[mine, lanes], topz_recv)
        for n, d in enumerate(away):
            push(top.at[mine, lanes], top.at[mine, lanes], top_send.at[7 + n], top_recv.at[col], row, at_col(*d))

    def top_swap():
        lanes = top_half(core)
        for d in away:
            source = at_col(*d)
            landed(top.at[strip_of(source), lanes], top_recv.at[source])
        push(top.at[:, lanes], top.at[:, lanes], top_send.at[22], topx_recv, other, col)

    def code_panel():
        for j in range(ROWS // 128):
            lanes = slice(128 * j, 128 * j + 128)
            v = panel[:, lanes]
            most = jnp.maximum(jnp.max(jnp.abs(v), axis=0, keepdims=True), 1e-30)
            step = most * (1.0 / 32760.0)
            coded[:, lanes] = jnp.round(v * (1.0 / step)).astype(jnp.int32).astype(jnp.int16)
            scales[j:j + 1, :] = step
            ps_scales[j // 4, j % 4:j % 4 + 1, :] = step
            ps_scales[j // 4, j % 4 + 4:j % 4 + 5, :] = step

    def ps_out(v, g):
        to_col = v + 9 * g
        unit = v + 1 - g
        part = coded.at[:, pl.ds(PANEL * unit, PANEL)]
        return (
            (part, ps_code.at[mine], ps_send.at[0, v], ps_recv.at[0, col], row, to_col),
            (ps_scales.at[unit], ps_scale.at[col], ps_send.at[1, v], ps_recv.at[1, col], row, to_col),
        )

    ps_pairs = [(v, g) for v in range(9) for g in range(2) if v + 9 * g < NC]

    def ps_first():
        for v, g in ps_pairs:
            @pl.when((row == g) & (col != v + 9 * g))
            def _():
                for args in ps_out(v, g):
                    remote(*args).start()

            @pl.when((row == g) & (col == v + 9 * g))
            def _():
                for args in ps_out(v, g):
                    pltpu.make_async_copy(args[0], args[1], args[3]).start()

    root = jnp.where(col < 9, 0, 1)

    def ps_copies(n, d):
        return (
            remote(ps_code, ps_code, psb_send.at[0, n], psb_recv.at[0], at_row(*d), col),
            remote(ps_scale, ps_scale, psb_send.at[1, n], psb_recv.at[1], at_row(*d), col),
        )

    from_root = list(enumerate(((1, 0), (3, 0), (2, 0), (0, 1))))

    def ps_second():
        @pl.when(row == root)
        def _():
            for d in plane:
                source = at_col(*d)
                landed(ps_code.at[strip_of(source)], ps_recv.at[0, source])
                landed(ps_scale.at[source], ps_recv.at[1, source])
            for n, d in from_root:
                for copy in ps_copies(n, d):
                    copy.start()

    def ps_third():
        @pl.when(row != root)
        def _():
            landed(ps_code, psb_recv.at[0])
            landed(ps_scale, psb_recv.at[1])

        @pl.when((core == root) & (z > 0))
        def _():
            for copy in ps_copies(3, (0, 1)):
                copy.start()

    halves = [pl.ds(0, HALF), pl.ds(HALF, HALF)]

    def along(h, n, m):
        return at_col(n, m) if h == 0 else at_col(m, n)

    def gather_first():
        pltpu.make_async_copy(scales, scale.at[col], s_recv.at[col]).start()
        for h in range(2):
            part = coded.at[:, halves[h]]
            pltpu.make_async_copy(part, code.at[mine, halves[h]], g_recv.at[h, col]).start()
            for n in (1, 3, 2):
                push(part, code.at[mine, halves[h]], g_send.at[h, n - 1], g_recv.at[h, col], row, along(h, n, 0))
        for n, d in enumerate(away):
            push(scales, scale.at[col], s_send.at[n], s_recv.at[col], row, at_col(*d))

    def gather_second():
        for n in range(4):
            for h in range(2):
                source = along(h, n, 0)
                part = code.at[strip_of(source), halves[h]]
                landed(part, g_recv.at[h, source])
                for m in (1, 3):
                    push(part, part, g_send.at[h, 3 + 2 * n + m // 2], g_recv.at[h, source], row, along(h, 0, m))

    def quarter(h, q):
        return pl.ds(HALF * h + HALF // 2 * q, HALF // 2)

    def gather_third():
        for n in range(4):
            for h in range(2):
                for q, m in enumerate((3, 1)):
                    source = along(h, n, m)
                    landed(code.at[strip_of(source), halves[h]], g_recv.at[h, source])
                    part = code.at[strip_of(source), quarter(h, q)]
                    to = along(h, 0, 1 if q == 0 else 3)
                    push(part, part, g_send.at[h, 11 + 2 * n + q], g3_recv.at[h, n, q], row, to)

    blk = lax.broadcasted_iota(jnp.int32, (PANEL, PANEL), 1) // 128
    eye = (
        lax.broadcasted_iota(jnp.int32, (128, PANEL), 0)
        == lax.broadcasted_iota(jnp.int32, (128, PANEL), 1) % 128
    ).astype(F32)

    def factor_start():
        landed(top.at[:, top_half(1 - core)], topx_recv)
        work[...] = top[...]

    def factor_step(k):
        rows = slice(128 * k, 128 * k + 128)
        for h, part in enumerate(eliminate(work[rows, rows])):
            inverse[8 * h:8 * h + 8, :] = part
        entry = jnp.where(blk[:128] == k, eye, work[rows, :])
        done = jnp.dot(inverse[...], entry, precision=HIGHEST, preferred_element_type=F32)
        work[rows, :] = done
        if k < 3:
            rest = slice(128 * k + 128, PANEL)
            count = PANEL - 128 * k - 128
            work[rest, :] = jnp.where(blk[:count] == k, 0.0, work[rest, :]) - lax.dot_general(
                done[:, rest], done, (((0,), (0,)), ((), ())),
                precision=HIGHEST, preferred_element_type=F32,
            )

    def factor_end():
        lower = lax.broadcasted_iota(jnp.int32, (PANEL, PANEL), 0) >= lax.broadcasted_iota(
            jnp.int32, (PANEL, PANEL), 1
        )
        work[...] = jnp.where(lower, work[...], 0.0)
        own_high[...], own_low[...] = halve(work[mine, :])

    def weights():
        for c in range(NC):
            part = slice(STRIP * c, STRIP * c + STRIP)
            for j in range(4):
                lanes = slice(128 * j, 128 * j + 128)
                rows_ps[part, lanes] = ps_code[part, lanes].astype(jnp.int32).astype(F32) * ps_scale[c, j:j + 1, :]
        half = jnp.dot(work[...], rows_ps[...], precision=HIGHEST, preferred_element_type=F32)
        w_high[...], w_low[...] = halve(
            lax.dot_general(
                work[...], half, (((0,), (0,)), ((), ())), precision=HIGHEST, preferred_element_type=F32
            )
        )

    columns_hop(0)
    slab_load.start()
    top_hop()
    columns_hop(1)
    code_panel()
    gather_first()
    ps_first()
    top_swap()
    rows_hop(0)
    factor_start()
    factor_step(0)
    gather_second()
    factor_step(1)
    rows_hop(1)
    ps_second()
    factor_step(2)
    gather_third()
    factor_step(3)
    ps_third()
    factor_end()
    weights()

    landed(scale.at[col], s_recv.at[col])
    for d in away:
        landed(scale.at[at_col(*d)], s_recv.at[at_col(*d)])
    for h in range(2):
        for n in range(4):
            source = along(h, n, 2)
            for q in range(2):
                landed(code.at[strip_of(source), quarter(h, q)], g3_recv.at[h, n, q])
    for s in range(NS):
        for dz, dk in line:
            k, from_z = (core + dk) % 2, (z + dz) % 4
            landed(arrived.at[k, from_z, s], c2_recv.at[s, from_z, k])
    slab_load.wait()
    for copy in sends:
        copy.wait_send()

    @pl.when(row == 0)
    def _():
        for n, d in enumerate(line_away):
            top_out(n, d).wait_send()

    for v, g in ps_pairs:
        @pl.when((row == g) & (col != v + 9 * g))
        def _():
            for args in ps_out(v, g):
                remote(*args).wait_send()

    @pl.when(row == root)
    def _():
        for n, d in from_root:
            for copy in ps_copies(n, d):
                copy.wait_send()

    @pl.when((core == root) & (z > 0))
    def _():
        for copy in ps_copies(3, (0, 1)):
            copy.wait_send()


def exchange(slots, panel, child_one, child_two, slab):
    vmem = pl.BlockSpec(memory_space=pltpu.VMEM)
    hbm = pl.BlockSpec(memory_space=pltpu.HBM)
    dma = pltpu.SemaphoreType.DMA
    return pl.pallas_call(
        exchange_kernel,
        out_shape=(
            jax.ShapeDtypeStruct((PANEL, ROWS), jnp.int16),
            jax.ShapeDtypeStruct((NC, ROWS // 128, 128), F32),
            jax.ShapeDtypeStruct((2, 4, NS, CAP, SUB, 128), BF16),
            jax.ShapeDtypeStruct((ROWS, WIDTH), F32),
            jax.ShapeDtypeStruct((PANEL, WIDTH), BF16),
            jax.ShapeDtypeStruct((PANEL, WIDTH), BF16),
            jax.ShapeDtypeStruct((STRIP, PANEL), BF16),
            jax.ShapeDtypeStruct((STRIP, PANEL), BF16),
        ),
        in_specs=[pl.BlockSpec(memory_space=pltpu.SMEM)] + [vmem] * 3 + [hbm],
        out_specs=(vmem,) * 8,
        scratch_shapes=[
            pltpu.VMEM((NS, 2, NC, SUB, 128), BF16),
            pltpu.VMEM((NS, NC, 2, SUB, 128), BF16),
            pltpu.VMEM((NS, 2 * NC, SUB, 128), BF16),
            pltpu.VMEM((NS, NR, CAP, SUB, 128), BF16),
            pltpu.VMEM((STRIP, ROWS), jnp.int16),
            pltpu.VMEM((ROWS // 128, 128), F32),
            pltpu.VMEM((ROWS // PANEL, 8, 128), F32),
            pltpu.VMEM((PANEL, PANEL), F32),
            pltpu.VMEM((PANEL, WIDTH), jnp.int16),
            pltpu.VMEM((NC, 8, 128), F32),
            pltpu.VMEM((PANEL, PANEL), F32),
            pltpu.VMEM((128, 128), F32),
            pltpu.VMEM((PANEL, WIDTH), F32),
            dma(()),
            dma((23,)), dma(()), dma((NC,)), dma(()),
            dma((NS, NC, 2)), dma((NS, NC, 2)),
            dma((NS, NR)), dma((NS, 4, 2)),
            dma((2, 19)), dma((2, NC)), dma((2, 4, 2)),
            dma((15,)), dma((NC,)),
            dma((2, 9)), dma((2, NC)),
            dma((2, 4)), dma((2,)),
        ],
        compiler_params=pltpu.CompilerParams(
            collective_id=0, has_side_effects=True, vmem_limit_bytes=26 * 1024 * 1024
        ),
    )(slots, panel, child_one, child_two, slab)


STEP = 512


def update_kernel(
    where, has, slab, code, scale, arrived, w_high, w_low, own_high, own_low, out, factor, rows_t,
):
    i = pl.program_id(0)
    row = lax.axis_index("row")
    tiles = STEP // 128
    for j in range(tiles):
        lanes = pl.ds(pl.multiple_of(i * STEP + 128 * j, 128), 128)
        for c in range(NC):
            part = slice(STRIP * c, STRIP * c + STRIP)
            rows_t[part, 128 * j:128 * j + 128] = (
                code[part, lanes].astype(jnp.int32).astype(F32) * scale[c, pl.ds(tiles * i + j, 1), :]
            )
    high, low = halve(rows_t[...])

    def dot(a, b):
        return jnp.dot(a, b, preferred_element_type=F32)

    factor[...] = dot(own_high[...], high) + dot(own_high[...], low) + dot(own_low[...], high)
    high, low = high.T, low.T
    update = dot(high, w_high[...]) + dot(low, w_high[...]) + dot(high, w_low[...])
    keep = (row * (ROWS // STEP) + i) >= PANEL // STEP
    update = jnp.where(keep, update, 0.0)
    for n in range(STEP // BLK):
        block = i * (STEP // BLK) + n
        one_at, two_at = where[block], where[ROWS // BLK + block]
        one_in, two_in = has[block] > 0, has[ROWS // BLK + block] > 0
        for s in range(NS):
            rows = slice(BLK * n + SUB * s, BLK * n + SUB * s + SUB)
            here = pl.ds(pl.multiple_of(i * STEP + BLK * n + SUB * s, SUB), SUB)
            for a in range(4):
                lanes = slice(128 * a, 128 * a + 128)
                one = jnp.where(one_in, arrived[0, a, s, one_at].astype(F32), 0.0)
                two = jnp.where(two_in, arrived[1, a, s, two_at].astype(F32), 0.0)
                out[rows, lanes] = ((slab[here, lanes] + one) + two) - update[rows, lanes]


def update(where, has, slab, code, scale, arrived, w_high, w_low, own_high, own_low):
    vmem = pl.BlockSpec(memory_space=pltpu.VMEM)
    return pl.pallas_call(
        update_kernel,
        grid_spec=pltpu.PrefetchScalarGridSpec(
            num_scalar_prefetch=2,
            grid=(ROWS // STEP,),
            in_specs=[vmem] * 8,
            out_specs=[
                pl.BlockSpec((STEP, WIDTH), lambda i, w, h: (i, 0)),
                pl.BlockSpec((STRIP, STEP), lambda i, w, h: (0, i)),
            ],
            scratch_shapes=[pltpu.VMEM((PANEL, STEP), F32)],
        ),
        out_shape=(
            jax.ShapeDtypeStruct((ROWS, WIDTH), F32),
            jax.ShapeDtypeStruct((STRIP, ROWS), F32),
        ),
        compiler_params=pltpu.CompilerParams(vmem_limit_bytes=16 * 1024 * 1024),
    )(where, has, slab, code, scale, arrived, w_high, w_low, own_high, own_low)


def routing(maps):
    steps = ROWS // BLK
    owner = maps // steps
    count = maps.shape[1]
    before = jnp.arange(count)[None, :] < jnp.arange(count)[:, None]
    same = owner[:, :, None] == owner[:, None, :]
    rank = jnp.sum((same & before[None]).astype(jnp.int32), 2)
    slot = owner * CAP + rank
    hit = slot[:, None, :] == jnp.arange(NR * CAP)[None, :, None]
    slots = jnp.sum(jnp.where(hit, jnp.arange(count)[None, None, :], 0), 2)
    mine = lax.axis_index("row") * steps + jnp.arange(steps)
    at = maps[:, None, :] == mine[None, :, None]
    where = jnp.sum(jnp.where(at, rank[:, None, :], 0), 2)
    has = jnp.sum(at.astype(jnp.int32), 2)
    return tuple(v.reshape(-1).astype(jnp.int32) for v in (slots, where, has))


def per_device(front_panel, front_slab, child_one, child_two, map_one, map_two):
    slots, where, has = routing(jnp.stack([map_one, map_two]))
    code, scale, arrived, slab, *parts = exchange(slots, front_panel.T, child_one, child_two, front_slab)
    slab, factor = update(where, has, slab, code, scale, arrived, *parts)
    return (factor.T, slab)


def solution(mesh):
    in_specs = (P("row", "col"), P("row", "col"), P("col", "row"), P("col", "row"), P(), P())
    out_specs = (P("row", "col"), P("row", "col"))
    return jax.shard_map(
        per_device, mesh=mesh, in_specs=in_specs, out_specs=out_specs, check_vma=False
    )
```

time: 228 us -> 123 us (0.54)
  the two profiles are of different devices: /device:TPU:16 before, /device:TPU:69 now
where the time goes in v2:
time: 123 us; the launch traced here: 122 us
  Pallas kernels  116 us (94%)
  local copies, waits for them, and re-layouts  3.97 us (3%)
  other arithmetic  1.81 us (1%)
    pallas_call x1, Pallas kernels, exchange(): pl.pallas_call(exchange_kernel, out_shape=(jax.ShapeDtypeStruct((PANEL, R...  99.7 us
    pallas_call x1, Pallas kernels, update(): pl.pallas_call(update_kernel, grid_spec=pltpu.PrefetchScalarGridSpec(num_...  16.2 us
    unnamed x6, local copies, waits for them, and re-layouts  3.54 us

profile of v2, /device:TPU:69, one launch (start us, length us, event | category | flops | bytes accessed | tf_op | source)
XLA Modules:
  0.0 122.4 jit_solution(13380690512581981005)
XLA Ops:
  0.6 0.7 and_select_fusion
  1.4 0.2 convert_reduce_fusion
  1.5 0.1 select_reduce_fusion
  1.6 0.1 reshape.161.slots
  1.7 0.8 fusion.1
  2.5 0.1 copy.9
  2.6 0.1 reshape.160.has
  2.7 0.1 copy.8
  2.8 0.1 reshape.159.where
  2.9 0.0 copy-start
  2.9 1.2 %copy-done = bf16[512,1024]{1,0:T(8,128)(2,1)S(1)} copy-done((bf16[512,1024]{1,0:T(8,128)(2,1)S(1)}, bf16[512,1024]{1,0:T(8,128)(2,1)}, u32[]{:S(2)}) %copy-start) | copy-done | bytes 1048600
  4.1 0.0 copy-start.1
  4.1 1.2 copy-done.1
  5.3 0.0 copy-start.2
  5.4 1.1 copy-done.2
  6.4 99.7 %shard_map.77 = (s16[512,5120]{1,0:T(8,128)(2,1)S(1)}, f32[16,40,128]{2,1,0:T(8,128)S(1)}, bf16[2,4,2,8,128,128]{5,4,3,2,1,0:T(8,128)(2,1)S(1)}, f32[5120,512]{1...) custom-call(s32[128]{0:T(128)S(1)} %reshape.161.slots, ...), custom_call_target="tpu_custom_call" | custom-call | tf_op jit(solution)/shard_map/pallas_call | solution.py:414
  106.2 16.2 %shard_map.78 = (f32[5120,512]{1,0:T(8,128)}, f32[32,5120]{1,0:T(8,128)}) custom-call(s32[40]{0:T(128)S(1)} %reshape.159.where, s32[40]{0:T(128)S(1)} %reshape.160.has, f32[5120,512]{1,0:T(8,128)S(1)} %get-tuple-element.12.slab, s16[512,5120]{1,0:T(8,128)(2,1)S(1)} %get-tuple-element.13.code, f32[16,40,128]{2,1,0:T(8,128)S(1)} %get-tuple-element.14.scale, ...), custom_call_target="tpu_custom_call" | custom-call | tf_op jit(solution)/shard_map/pallas_call | solution.py:499
  (3 shorter events, 0.0 us)
Async XLA Ops:
  2.9 1.2 %copy-start = (bf16[512,1024]{1,0:T(8,128)(2,1)S(1)}, bf16[512,1024]{1,0:T(8,128)(2,1)}, u32[]{:S(2)}) copy-start(bf16[512,1024]{1,0:T(8,128)(2,1)} %child_one.1) | copy-start | bytes 3145732
  4.1 1.2 %copy-start.1 = (bf16[512,1024]{1,0:T(8,128)(2,1)S(1)}, bf16[512,1024]{1,0:T(8,128)(2,1)}, u32[]{:S(2)}) copy-start(bf16[512,1024]{1,0:T(8,128)(2,1)} %child_two.1) | copy-start | bytes 3145732
  5.3 1.1 copy-start.2

commit v3 on v2

--- a/solution.py
+++ b/solution.py
@@ -16,8 +16,9 @@
 HALF = ROWS // 2
 WIDTH = 512
 CAP = 8
-NS = 2
+NS = 4
 SUB = BLK // NS
+STEP = 512
 MESH = pl.DeviceIdType.MESH
 F32 = jnp.float32
 BF16 = jnp.bfloat16
@@ -77,8 +78,8 @@
 
 def exchange_kernel(
     slots, panel, child_one, child_two, slab_hbm,
-    code, scale, arrived, slab, w_high, w_low, own_high, own_low,
-    pack, got, blocks, outgoing, coded, scales, ps_scales,
+    arrived, slab, factor,
+    code, scale, w_high, w_low, own_high, own_low, rows_t, pack, got, blocks, outgoing, coded, scales, ps_scales,
     top, ps_code, ps_scale, work, inverse, rows_ps,
     load, top_send, topz_recv, top_recv, topx_recv, c1_send, c1_recv, c2_send, c2_recv,
     g_send, g_recv, g3_recv, s_send, s_recv, ps_send, ps_recv, psb_send, psb_recv,
@@ -114,8 +115,6 @@
     for dz in range(1, 4):
         for dk in range(2):
             pl.semaphore_signal(barrier, inc=1, device_id=(at_row(dz, dk), col), device_id_type=MESH)
-    pl.semaphore_wait(barrier, 37)
-
     sends = []
 
     def remote(src, dst, send, recv, to_row, to_col):
@@ -139,15 +138,16 @@
         lanes = pl.ds(256 * d[1], 256)
         return remote(panel.at[:, lanes], top.at[mine, lanes], top_send.at[n], topz_recv, at_row(*d), col)
 
-    @pl.when(row == 0)
-    def _():
-        for n, d in enumerate(line_away):
-            top_out(n, d).start()
-        pltpu.make_async_copy(panel.at[:, pl.ds(0, 256)], top.at[mine, pl.ds(0, 256)], topz_recv).start()
+    def top_first():
+        @pl.when(row == 0)
+        def _():
+            for n, d in enumerate(line_away):
+                top_out(n, d).start()
+            pltpu.make_async_copy(panel.at[:, pl.ds(0, 256)], top.at[mine, pl.ds(0, 256)], topz_recv).start()
 
     low = lax.broadcasted_iota(jnp.int32, (SUB, 128), 1) < 64
 
-    def columns_hop(s):
+    def columns_pack(s):
         for t, child in enumerate((child_one, child_two)):
             for p in range(NC // 2):
                 lanes = slice(128 * p, 128 * p + 128)
@@ -155,6 +155,8 @@
                 second = child[BLK + s * SUB:BLK + (s + 1) * SUB, lanes]
                 pack[s, t, 2 * p] = jnp.where(low, first, swap_halves(second))
                 pack[s, t, 2 * p + 1] = jnp.where(low, swap_halves(first), second)
+
+    def columns_hop(s):
         for n, d in enumerate(plane):
             for dk in range(2):
                 to = (core + dk) % 2
@@ -301,6 +303,16 @@
                     to = along(h, 0, 1 if q == 0 else 3)
                     push(part, part, g_send.at[h, 11 + 2 * n + q], g3_recv.at[h, n, q], row, to)
 
+    def gather_end():
+        landed(scale.at[col], s_recv.at[col])
+        for d in away:
+            landed(scale.at[at_col(*d)], s_recv.at[at_col(*d)])
+        for h in range(2):
+            for n in range(4):
+                source = along(h, n, 2)
+                for q in range(2):
+                    landed(code.at[strip_of(source), quarter(h, q)], g3_recv.at[h, n, q])
+
     blk = lax.broadcasted_iota(jnp.int32, (PANEL, PANEL), 1) // 128
     eye = (
         lax.broadcasted_iota(jnp.int32, (128, PANEL), 0)
@@ -346,41 +358,70 @@
             )
         )
 
+    def dot(a, b):
+        return jnp.dot(a, b, preferred_element_type=F32)
+
+    def update_rows():
+        tiles = STEP // 128
+
+        def step(i, carry):
+            for j in range(tiles):
+                lanes = pl.ds(pl.multiple_of(i * STEP + 128 * j, 128), 128)
+                for c in range(NC):
+                    part = slice(STRIP * c, STRIP * c + STRIP)
+                    rows_t[part, 128 * j:128 * j + 128] = (
+                        code[part, lanes].astype(jnp.int32).astype(F32) * scale[c, pl.ds(tiles * i + j, 1), :]
+                    )
+            here = pl.ds(pl.multiple_of(i * STEP, STEP), STEP)
+            high, low = halve(rows_t[...])
+            factor[:, here] = dot(own_high[...], high) + dot(own_high[...], low) + dot(own_low[...], high)
+            high, low = high.T, low.T
+            update = dot(high, w_high[...]) + dot(low, w_high[...]) + dot(high, w_low[...])
+            keep = (row * (ROWS // STEP) + i) >= PANEL // STEP
+            slab[here, :] = slab[here, :] - jnp.where(keep, update, 0.0)
+            return carry
+
+        lax.fori_loop(0, ROWS // STEP, step, 0)
+
+    columns_pack(0)
+    code_panel()
+    pl.semaphore_wait(barrier, 37)
+    top_first()
+    ps_first()
     columns_hop(0)
     slab_load.start()
+    columns_pack(1)
+    columns_hop(1)
     top_hop()
-    columns_hop(1)
-    code_panel()
+    columns_pack(2)
+    columns_hop(2)
+    ps_second()
+    columns_pack(3)
+    columns_hop(3)
+    rows_hop(0)
     gather_first()
-    ps_first()
     top_swap()
-    rows_hop(0)
+    rows_hop(1)
+    ps_third()
     factor_start()
     factor_step(0)
     gather_second()
+    rows_hop(2)
     factor_step(1)
-    rows_hop(1)
-    ps_second()
+    rows_hop(3)
+    gather_third()
     factor_step(2)
-    gather_third()
     factor_step(3)
-    ps_third()
     factor_end()
     weights()
-
-    landed(scale.at[col], s_recv.at[col])
-    for d in away:
-        landed(scale.at[at_col(*d)], s_recv.at[at_col(*d)])
-    for h in range(2):
-        for n in range(4):
-            source = along(h, n, 2)
-            for q in range(2):
-                landed(code.at[strip_of(source), quarter(h, q)], g3_recv.at[h, n, q])
+    gather_end()
+    slab_load.wait()
+    update_rows()
+
     for s in range(NS):
         for dz, dk in line:
             k, from_z = (core + dk) % 2, (z + dz) % 4
             landed(arrived.at[k, from_z, s], c2_recv.at[s, from_z, k])
-    slab_load.wait()
     for copy in sends:
         copy.wait_send()
 
@@ -414,18 +455,20 @@
     return pl.pallas_call(
         exchange_kernel,
         out_shape=(
-            jax.ShapeDtypeStruct((PANEL, ROWS), jnp.int16),
-            jax.ShapeDtypeStruct((NC, ROWS // 128, 128), F32),
             jax.ShapeDtypeStruct((2, 4, NS, CAP, SUB, 128), BF16),
             jax.ShapeDtypeStruct((ROWS, WIDTH), F32),
-            jax.ShapeDtypeStruct((PANEL, WIDTH), BF16),
-            jax.ShapeDtypeStruct((PANEL, WIDTH), BF16),
-            jax.ShapeDtypeStruct((STRIP, PANEL), BF16),
-            jax.ShapeDtypeStruct((STRIP, PANEL), BF16),
+            jax.ShapeDtypeStruct((STRIP, ROWS), F32),
         ),
         in_specs=[pl.BlockSpec(memory_space=pltpu.SMEM)] + [vmem] * 3 + [hbm],
-        out_specs=(vmem,) * 8,
+        out_specs=(vmem,) * 3,
         scratch_shapes=[
+            pltpu.VMEM((PANEL, ROWS), jnp.int16),
+            pltpu.VMEM((NC, ROWS // 128, 128), F32),
+            pltpu.VMEM((PANEL, WIDTH), BF16),
+            pltpu.VMEM((PANEL, WIDTH), BF16),
+            pltpu.VMEM((STRIP, PANEL), BF16),
+            pltpu.VMEM((STRIP, PANEL), BF16),
+            pltpu.VMEM((PANEL, STEP), F32),
             pltpu.VMEM((NS, 2, NC, SUB, 128), BF16),
             pltpu.VMEM((NS, NC, 2, SUB, 128), BF16),
             pltpu.VMEM((NS, 2 * NC, SUB, 128), BF16),
@@ -449,37 +492,14 @@
             dma((2, 4)), dma((2,)),
         ],
         compiler_params=pltpu.CompilerParams(
-            collective_id=0, has_side_effects=True, vmem_limit_bytes=26 * 1024 * 1024
+            collective_id=0, has_side_effects=True, vmem_limit_bytes=36 * 1024 * 1024
         ),
     )(slots, panel, child_one, child_two, slab)
 
 
-STEP = 512
-
-
-def update_kernel(
-    where, has, slab, code, scale, arrived, w_high, w_low, own_high, own_low, out, factor, rows_t,
-):
+def place_kernel(where, has, slab, factor, arrived, out, factor_out):
     i = pl.program_id(0)
-    row = lax.axis_index("row")
-    tiles = STEP // 128
-    for j in range(tiles):
-        lanes = pl.ds(pl.multiple_of(i * STEP + 128 * j, 128), 128)
-        for c in range(NC):
-            part = slice(STRIP * c, STRIP * c + STRIP)
-            rows_t[part, 128 * j:128 * j + 128] = (
-                code[part, lanes].astype(jnp.int32).astype(F32) * scale[c, pl.ds(tiles * i + j, 1), :]
-            )
-    high, low = halve(rows_t[...])
-
-    def dot(a, b):
-        return jnp.dot(a, b, preferred_element_type=F32)
-
-    factor[...] = dot(own_high[...], high) + dot(own_high[...], low) + dot(own_low[...], high)
-    high, low = high.T, low.T
-    update = dot(high, w_high[...]) + dot(low, w_high[...]) + dot(high, w_low[...])
-    keep = (row * (ROWS // STEP) + i) >= PANEL // STEP
-    update = jnp.where(keep, update, 0.0)
+    factor_out[...] = factor[...]
     for n in range(STEP // BLK):
         block = i * (STEP // BLK) + n
         one_at, two_at = where[block], where[ROWS // BLK + block]
@@ -491,29 +511,26 @@
                 lanes = slice(128 * a, 128 * a + 128)
                 one = jnp.where(one_in, arrived[0, a, s, one_at].astype(F32), 0.0)
                 two = jnp.where(two_in, arrived[1, a, s, two_at].astype(F32), 0.0)
-                out[rows, lanes] = ((slab[here, lanes] + one) + two) - update[rows, lanes]
-
-
-def update(where, has, slab, code, scale, arrived, w_high, w_low, own_high, own_low):
+                out[rows, lanes] = (slab[here, lanes] + one) + two
+
+
+def place(where, has, slab, factor, arrived):
     vmem = pl.BlockSpec(memory_space=pltpu.VMEM)
+    part = pl.BlockSpec((STRIP, STEP), lambda i, w, h: (0, i))
     return pl.pallas_call(
-        update_kernel,
+        place_kernel,
         grid_spec=pltpu.PrefetchScalarGridSpec(
             num_scalar_prefetch=2,
             grid=(ROWS // STEP,),
-            in_specs=[vmem] * 8,
-            out_specs=[
-                pl.BlockSpec((STEP, WIDTH), lambda i, w, h: (i, 0)),
-                pl.BlockSpec((STRIP, STEP), lambda i, w, h: (0, i)),
-            ],
-            scratch_shapes=[pltpu.VMEM((PANEL, STEP), F32)],
+            in_specs=[vmem, part, vmem],
+            out_specs=[pl.BlockSpec((STEP, WIDTH), lambda i, w, h: (i, 0)), part],
         ),
         out_shape=(
             jax.ShapeDtypeStruct((ROWS, WIDTH), F32),
             jax.ShapeDtypeStruct((STRIP, ROWS), F32),
         ),
         compiler_params=pltpu.CompilerParams(vmem_limit_bytes=16 * 1024 * 1024),
-    )(where, has, slab, code, scale, arrived, w_high, w_low, own_high, own_low)
+    )(where, has, slab, factor, arrived)
 
 
 def routing(maps):
@@ -535,8 +552,8 @@
 
 def per_device(front_panel, front_slab, child_one, child_two, map_one, map_two):
     slots, where, has = routing(jnp.stack([map_one, map_two]))
-    code, scale, arrived, slab, *parts = exchange(slots, front_panel.T, child_one, child_two, front_slab)
-    slab, factor = update(where, has, slab, code, scale, arrived, *parts)
+    arrived, slab, factor = exchange(slots, front_panel.T, child_one, child_two, front_slab)
+    slab, factor = place(where, has, slab, factor, arrived)
     return (factor.T, slab)
 
 

time: 123 us -> 113 us (0.919)
  the two profiles are of different devices: /device:TPU:69 before, /device:TPU:16 now
where the time goes in v3:
time: 113 us
  Pallas kernels  107 us (95%)
  local copies, waits for them, and re-layouts  3.97 us (4%)
  other arithmetic  1.81 us (2%)
    pallas_call x1, Pallas kernels, exchange(): pl.pallas_call(exchange_kernel, out_shape=(jax.ShapeDtypeStruct((2, 4, NS...  99.8 us
    pallas_call x1, Pallas kernels, place(): pl.pallas_call(place_kernel, grid_spec=pltpu.PrefetchScalarGridSpec(num_s...  6.87 us
    unnamed x6, local copies, waits for them, and re-layouts  3.54 us

profile of v3, /device:TPU:16, one launch (start us, length us, event | category | flops | bytes accessed | tf_op | source)
XLA Modules:
  0.0 113.1 jit_solution(17382452398861238211)
XLA Ops:
  0.6 0.7 and_select_fusion
  1.4 0.2 convert_reduce_fusion
  1.5 0.1 select_reduce_fusion
  1.6 0.1 reshape.161.slots
  1.7 0.8 fusion.1
  2.5 0.1 copy.9
  2.6 0.1 reshape.160.has
  2.7 0.1 copy.8
  2.8 0.1 reshape.159.where
  2.9 0.0 copy-start
  2.9 1.2 %copy-done = bf16[512,1024]{1,0:T(8,128)(2,1)S(1)} copy-done((bf16[512,1024]{1,0:T(8,128)(2,1)S(1)}, bf16[512,1024]{1,0:T(8,128)(2,1)}, u32[]{:S(2)}) %copy-start) | copy-done | bytes 1048600
  4.1 0.0 copy-start.1
  4.1 1.2 %copy-done.1 = bf16[512,1024]{1,0:T(8,128)(2,1)S(1)} copy-done((bf16[512,1024]{1,0:T(8,128)(2,1)S(1)}, bf16[512,1024]{1,0:T(8,128)(2,1)}, u32[]{:S(2)}) %copy-start.1) | copy-done | bytes 1048600
  5.3 0.0 copy-start.2
  5.4 1.1 copy-done.2
  6.4 99.8 %shard_map.77 = (bf16[2,4,4,8,64,128]{5,4,3,2,1,0:T(8,128)(2,1)S(1)}, f32[5120,512]{1,0:T(8,128)S(1)}, f32[32,5120]{1,0:T(8,128)S(1)}) custom-call(s32[128]{0:T(128)S(1)} %reshape.161.slots, f32[32,5120]{1,0:T(8,128)S(1)} %bitcast.4, bf16[512,1024]{1,0:T(8,128)(2,1)S(1)} %copy-done, bf16[512,1024]{1,0:T(8,128)(2,1)S(1)} %copy-done.1, f32[5120,512]{1,0:T(8,128)} %slab_hbm.1), custom_call_target="tpu_custom_call" | custom-call | tf_op jit(solution)/shard_map/pallas_call | solution.py:455
  106.2 6.9 %shard_map.78 = (f32[5120,512]{1,0:T(8,128)}, f32[32,5120]{1,0:T(8,128)}) custom-call(s32[40]{0:T(128)S(1)} %reshape.159.where, s32[40]{0:T(128)S(1)} %reshape.160.has, f32[5120,512]{1,0:T(8,128)S(1)} %get-tuple-element.7.slab, f32[32,5120]{1,0:T(8,128)S(1)} %get-tuple-element.8.factor, bf16[2,4,4,8,64,128]{5,4,3,2,1,0:T(8,128)(2,1)S(1)} %get-tuple-element.9.arrived), custom_call_target="tpu_custom_call" | custom-call | tf_op jit(solution)/shard_map/pallas_call | solution.py:520
  (3 shorter events, 0.0 us)
Async XLA Ops:
  2.9 1.2 %copy-start = (bf16[512,1024]{1,0:T(8,128)(2,1)S(1)}, bf16[512,1024]{1,0:T(8,128)(2,1)}, u32[]{:S(2)}) copy-start(bf16[512,1024]{1,0:T(8,128)(2,1)} %child_one.1) | copy-start | bytes 3145732
  4.1 1.2 %copy-start.1 = (bf16[512,1024]{1,0:T(8,128)(2,1)S(1)}, bf16[512,1024]{1,0:T(8,128)(2,1)}, u32[]{:S(2)}) copy-start(bf16[512,1024]{1,0:T(8,128)(2,1)} %child_two.1) | copy-start | bytes 3145732
  5.3 1.1 copy-start.2
